TPU v7x, 512 devices: a whole 4x4x16 slice. The times are simulated.
512 devices in a mesh: tm: 16 (over z_lo, y), space: 32 (over x, z_hi, core).
Axes of the slice: x: 4, y: 4, z: 16 (z_hi: 4, z_lo: 4; z = z_hi * 4 + z_lo), core: 2. Of those that a mesh axis runs over, the one named last changes fastest.
Arguments:
- residual: float32 [4, 1024, 16384], P(None, 'tm', 'space'), may hold values from -6 to 6
- members: int32 [64, 256], P('space'), may hold values from 0 to 16383, as said below
- eig_vectors: float32 [64, 256, 256], P('space'), may hold values from -0.375 to 0.375
- eig_left: float32 [64, 256, 256], P('space'), may hold values from -0.375 to 0.375
- eig_values: float32 [64, 256], P('space'), may hold values from 0.01 to 4
- compress: float32 [64, 32, 256], P('space'), may hold values from -0.375 to 0.375
- expand: float32 [64, 256, 32], P('space'), may hold values from -1 to 1
- neighbors: int32 [64, 8], P('space'), may hold values from 0 to 63
- coupling: float32 [64, 8], P('space'), may hold values from 0.1 to 0.4
Outputs:
- correction: float32 [4, 1024, 16384], P(None, 'tm', 'space')
Inputs may be any that keep to these rules, and one draw needn't show every extreme that they name: `members`: each row lists the 256 panels of one cluster and every panel appears exactly once; clusters k * 2 to (k + 1) * 2 - 1 together hold exactly the panels k * 2 * 256 to (k + 1) * 2 * 256 - 1.
All inputs are finite; a program needn't handle non-finite values.
Results may differ from a plain program's by a relative error of at most 0.0018.
Values may be sent and summed in bfloat16 or wider, within the bound.
A program may use at most 64 MiB of HBM per device.

v0:
```python
import math

import jax
import jax.numpy as jnp
from jax import lax
from jax.sharding import PartitionSpec as P


def forward_table(step_count, slot_count):
    freq_ids = lax.iota(jnp.int32, slot_count)[:, None]
    time_ids = lax.iota(jnp.int32, step_count)[None, :]
    phases = (freq_ids * time_ids % step_count).astype(jnp.float32) * (2.0 * math.pi / step_count)
    cosine = jnp.cos(phases)
    sine_part = -jnp.sin(phases)
    return jnp.stack([cosine, sine_part])


def inverse_table(step_count, slot_count):
    time_ids = lax.iota(jnp.int32, step_count)[:, None]
    freq_ids = lax.iota(jnp.int32, slot_count)[None, :]
    phases = (freq_ids * time_ids % step_count).astype(jnp.float32) * (2.0 * math.pi / step_count)
    cosine = jnp.cos(phases) / step_count
    sine_part = -jnp.sin(phases) / step_count
    return jnp.stack([cosine, sine_part])


def apply_gains(mode_real, mode_imag, freq_ids, step_count, lam):
    phases = (freq_ids % step_count).astype(jnp.float32) * (2.0 * math.pi / step_count)
    real_part = 1.0 - jnp.cos(phases) + lam
    shift_imag = jnp.sin(phases) + jnp.zeros_like(lam)
    modulus = real_part * real_part + shift_imag * shift_imag
    gain_real = real_part / modulus
    gain_imag = -shift_imag / modulus
    coef_ri = -gain_imag
    return (
        gain_real * mode_real + coef_ri * mode_imag,
        gain_imag * mode_real + gain_real * mode_imag,
    )


def on_device(
    residual, members, eig_vectors, eig_left, eig_values, compress, expand, neighbors, coupling
):
    highest = lax.Precision.HIGHEST
    sources, local_steps, panels_dev = residual.shape
    clusters_dev, panel_size = members.shape
    rank_size = compress.shape[1]
    time_devices = lax.axis_size("tm")
    step_count = local_steps * time_devices
    local_index = (members - lax.axis_index("space") * panels_dev).reshape(-1)
    ordered = jnp.take(residual, local_index, axis=2)
    forward = forward_table(step_count, step_count)
    backward = inverse_table(step_count, step_count)
    by_panel = lax.all_to_all(ordered, "tm", split_axis=2, concat_axis=1, tiled=True)
    spectrum = jnp.einsum("rtp,qkt->prqk", by_panel, forward, precision=highest)
    by_freq = lax.all_to_all(spectrum, "tm", split_axis=3, concat_axis=0, tiled=True)
    slots_dev = step_count // time_devices
    spectral = by_freq.reshape(clusters_dev, panel_size, sources, 2, slots_dev)
    in_modes = jnp.einsum("cij,cjrqk->cirqk", eig_left, spectral, precision=highest)
    freq_ids = (lax.axis_index("tm") * slots_dev + lax.iota(jnp.int32, slots_dev))[
        None, None, None, :
    ]
    lam = eig_values[:, :, None, None]
    new_real, new_imag = apply_gains(
        in_modes[:, :, :, 0], in_modes[:, :, :, 1], freq_ids, step_count, lam
    )
    scaled = jnp.stack([new_real, new_imag], 3)
    solved = jnp.einsum("cij,cjrqk->cirqk", eig_vectors, scaled, precision=highest)
    back_panels = lax.all_to_all(
        solved.reshape(panels_dev, sources, 2, slots_dev),
        "tm",
        split_axis=0,
        concat_axis=3,
        tiled=True,
    )
    panel_time = jnp.einsum("prqk,qtk->rtp", back_panels, backward, precision=highest)
    in_time = lax.all_to_all(panel_time, "tm", split_axis=1, concat_axis=2, tiled=True)
    columns = sources * local_steps
    grouped_time = in_time.reshape(sources, local_steps, clusters_dev, panel_size)
    summary = jnp.einsum("cmj,rtcj->cmrt", compress, grouped_time, precision=highest).astype(
        jnp.bfloat16
    )
    summary = summary.reshape(clusters_dev, rank_size * columns)
    block_part = lax.all_gather(summary, "space", axis=0, tiled=True)
    count_here = block_part.shape[0]
    row_ids = lax.iota(jnp.int32, count_here)
    selector = jnp.sum(
        jnp.where(neighbors[:, :, None] == row_ids[None, None, :], coupling[:, :, None], 0.0),
        axis=1,
    )
    mixed = jnp.dot(selector, block_part.astype(jnp.float32), precision=highest)
    mixed = mixed.reshape(clusters_dev, rank_size, sources, local_steps)
    adjusted = jnp.einsum("cim,cmrt->rtci", expand, mixed, precision=highest)
    result = in_time - adjusted.reshape(sources, local_steps, panels_dev)
    correction = jnp.zeros_like(result).at[:, :, local_index].set(result)
    return correction


def solution(mesh):
    return jax.shard_map(
        on_device,
        mesh=mesh,
        in_specs=(
            P(None, "tm", "space"),
            P("space", None),
            P("space", None, None),
            P("space", None, None),
            P("space", None),
            P("space", None, None),
            P("space", None, None),
            P("space", None),
            P("space", None),
        ),
        out_specs=P(None, "tm", "space"),
        check_vma=False,
    )
```

profile of v0, /device:TPU:1, one launch (start us, length us, event | category | flops | bytes accessed | tf_op | source)
XLA Modules:
  0.0 308.7 jit_solution(17070483956779373704)
XLA Ops:
  14.4 9.7 %all-to-all-start = ((f32[16,1,8192]{2,1,0:T(1,128)}), f32[16,1,8192]{2,1,0:T(1,128)S(1)}, u32[]{:S(2)}, u32[]{:S(2)}) async-start(f32[16,1,8192]{2,1,0:T(1,128)} %reshape.247), calls=%async_computation | async-start | bytes 1048576 | tf_op jit(solution)/shard_map/all_to_all | solution.py:54
  24.1 17.7 %sine_negate_fusion = (f32[1,1024,1024]{2,1,0:T(8,128)}, f32[1,1024,1024]{2,1,0:T(8,128)}) fusion(), kind=kLoop, calls=%fused_computation.16 | loop fusion | flops 15728640 | bytes 8388608 | tf_op jit(solution)/shard_map/neg | solution.py:23
  45.9 11.2 %fusion.18 = f32[32,4,2,1024]{3,0,1,2:T(8,128)S(1)} fusion(f32[4,1024,32,1]{1,2,0,3:T(8,128)S(1)} %reshape.238, f32[1,1024,1024]{2,1,0:T(8,128)} %get-tuple-element.12, f32[1,1024,1024]{2,1,0:T(8,128)} %get-tuple-element.13), kind=kOutput, calls=%fused_computation.26 | convolution fusion | flops 3223322624 | bytes 9961472 | tf_op jit(solution)/shard_map/rtp,qkt->prqk/dot_general | solution.py:55
  57.1 3.2 %copy.68 = f32[32,4,2,1024]{0,1,2,3:T(4,128)} copy(f32[32,4,2,1024]{3,0,1,2:T(8,128)S(1)} %fusion.18) | data formatting | bytes 2097152 | tf_op jit(solution)/shard_map/rtp,qkt->prqk/transpose | solution.py:55
  60.3 5.2 %reshape.249 = f32[16,1,16384]{2,1,0:T(1,128)} reshape(f32[1024,2,4,32]{3,2,1,0:T(4,128)} %bitcast.107) | data formatting | bytes 2097152
  65.5 7.2 %all-to-all-start.1 = ((f32[16,1,16384]{2,1,0:T(1,128)}), f32[16,1,16384]{2,1,0:T(1,128)S(1)}, u32[]{:S(2)}, u32[]{:S(2)}) async-start(f32[16,1,16384]{2,1,0:T(1,128)} %reshape.249), calls=%async_computation.1 | async-start | bytes 2097152 | tf_op jit(solution)/shard_map/all_to_all | solution.py:56
  73.0 21.9 %all-to-all-done.1 = f32[16,1,16384]{2,1,0:T(1,128)S(1)} async-done(((f32[16,1,16384]{2,1,0:T(1,128)}), f32[16,1,16384]{2,1,0:T(1,128)S(1)}, u32[]{:S(2)}, u32[]{:S(2)}) %all-to-all-start.1) | async-done | bytes 1048608 | tf_op jit(solution)/shard_map/all_to_all | solution.py:56
  94.8 3.1 %reduce.1 = f32[16,16384]{1,0:T(8,128)S(1)} reduce(f32[16,1,16384]{2,1,0:T(1,128)S(1)} %all-to-all-done.1, f32[]{:T(128)} %broadcast.345), dimensions={1}, to_apply=%all_to_all.54.reduce_sub_computation | reduce | bytes 2097156 | tf_op jit(solution)/shard_map/all_to_all | solution.py:56
  98.0 3.5 %reshape.250 = f32[1024,2,4,32]{3,2,1,0:T(4,128)} reshape(f32[16,16384]{1,0:T(8,128)S(1)} %reduce.1) | data formatting | bytes 2097152
  101.5 3.5 %copy.69 = f32[32,4,2,16,64]{4,0,3,2,1:T(8,128)S(1)} copy(f32[32,4,2,16,64]{0,1,2,4,3:T(4,128)} %bitcast.108) | data formatting | bytes 2097152 | tf_op jit(solution)/shard_map/all_to_all | solution.py:56
  105.1 3.4 %fusion.15 = f32[2,256,4,2,64]{1,4,3,2,0:T(8,128)S(1)} fusion(f32[2,256,4,2,64]{4,1,0,3,2:T(8,128)S(1)} %bitcast.110, f32[2,256,256]{2,1,0:T(8,128)S(1)} %copy-done), kind=kOutput, calls=%fused_computation.25 | convolution fusion | flops 805306368 | bytes 2621440 | tf_op jit(solution)/shard_map/cij,cjrqk->cirqk/dot_general | solution.py:59
  110.7 3.0 copy.95
  113.7 3.2 %reshape.251 = f32[16,1,16384]{2,1,0:T(1,128)} reshape(f32[512,4,2,64]{3,2,1,0:T(2,128)S(1)} %bitcast.113) | data formatting | bytes 2097152
  116.9 7.8 %all-to-all-start.2 = ((f32[16,1,16384]{2,1,0:T(1,128)}), f32[16,1,16384]{2,1,0:T(1,128)S(1)}, u32[]{:S(2)}, u32[]{:S(2)}) async-start(f32[16,1,16384]{2,1,0:T(1,128)} %reshape.251), calls=%async_computation.2 | async-start | bytes 2097152 | tf_op jit(solution)/shard_map/all_to_all | solution.py:69
  125.0 17.8 %broadcast_multiply_fusion = (f32[1,1024,1024]{2,1,0:T(8,128)}, f32[1,1024,1024]{2,1,0:T(8,128)}) fusion(), kind=kLoop, calls=%fused_computation.22 | loop fusion | flops 17825792 | bytes 8388608 | tf_op jit(solution)/shard_map/div | solution.py:23
  142.8 4.0 %all-to-all-done.2 = f32[16,1,16384]{2,1,0:T(1,128)S(1)} async-done(((f32[16,1,16384]{2,1,0:T(1,128)}), f32[16,1,16384]{2,1,0:T(1,128)S(1)}, u32[]{:S(2)}, u32[]{:S(2)}) %all-to-all-start.2) | async-done | bytes 1048608 | tf_op jit(solution)/shard_map/all_to_all | solution.py:69
  146.8 4.5 %reduce.2 = f32[16,16384]{1,0:T(8,128)} reduce(f32[16,1,16384]{2,1,0:T(1,128)S(1)} %all-to-all-done.2, f32[]{:T(128)} %broadcast.345), dimensions={1}, to_apply=%all_to_all.57.reduce_sub_computation | reduce | bytes 2097156 | tf_op jit(solution)/shard_map/all_to_all | solution.py:69
  151.3 2.7 reshape.252
  157.3 11.4 %fusion.19 = f32[4,1024,32]{1,2,0:T(8,128)S(1)} fusion(f32[32,4,2,1024]{3,0,2,1:T(8,128)} %all_to_all.60, f32[1,1024,1024]{2,1,0:T(8,128)} %get-tuple-element.16, f32[1,1024,1024]{2,1,0:T(8,128)} %get-tuple-element.17), kind=kOutput, calls=%fused_computation.28 | convolution fusion | flops 3223322624 | bytes 9961472 | tf_op jit(solution)/shard_map/prqk,qtk->rtp/dot_general | solution.py:76
  171.2 20.8 %all_to_all.69 = f32[16,1,8192]{2,1,0:T(1,128)S(1)} all-to-all(f32[16,1,8192]{2,1,0:T(1,128)S(1)} %reshape.253), channel_id=1, replica_groups=mesh['tm'=16,'space'=32] {'tm'}, dimensions={0} | all-to-all | bytes 1048576 | tf_op jit(solution)/shard_map/all_to_all | solution.py:77
  193.8 2.5 reshape.254
  199.9 75.2 %all-gather.3.cloned.1.call-done = bf16[32,2,8192]{2,1,0:T(2,128)(2,1)} async-done(((bf16[1,2,8192]{2,1,0:T(2,128)(2,1)}), bf16[32,2,8192]{2,1,0:T(2,128)(2,1)}) %all-gather.3.cloned.1.call-update) | async-done | bytes 1048592 | tf_op jit(solution)/shard_map/all_gather | solution.py:84
  278.4 6.5 %fusion.33 = f32[2,32,4,64]{3,0,2,1:T(2,128)S(1)} fusion(bf16[32,4,64,64]{3,2,1,0:T(8,128)(2,1)} %bitcast.114, f32[2,64]{1,0:T(2,128)S(1)} %select_reduce_fusion), kind=kOutput, calls=%fused_computation.61 | convolution fusion | flops 12582912 | bytes 1114624 | tf_op jit(solution)/shard_map/dot_general | solution.py:91
  286.9 13.6 %scatter_fusion = f32[4,64,512]{1,0,2:T(4,128)S(1)} fusion(f32[4,64,512]{1,0,2:T(4,128)S(1)} %broadcast_in_dim.24, s32[512]{0:T(512)S(1)} %bitcast.120, f32[512,4,64]{2,1,0:T(4,128)S(1)} %copy.83), kind=kCustom, calls=%fused_computation.1 | custom fusion | bytes 1574912 | tf_op jit(solution)/shard_map/scatter | solution.py:95
  (59 shorter events, 32.0 us)
Async XLA Ops:
  6.5 98.5 %copy-start = (f32[2,256,256]{2,1,0:T(8,128)S(1)}, f32[2,256,256]{2,1,0:T(8,128)}, u32[]{:S(2)}) copy-start(f32[2,256,256]{2,1,0:T(8,128)} %param.12) | copy-start | bytes 1572868
  14.4 27.4 %all-to-all-start = ((f32[16,1,8192]{2,1,0:T(1,128)}), f32[16,1,8192]{2,1,0:T(1,128)S(1)}, u32[]{:S(2)}, u32[]{:S(2)}) async-start(f32[16,1,8192]{2,1,0:T(1,128)} %reshape.247), calls=%async_computation | async-start | bytes 1048576 | tf_op jit(solution)/shard_map/all_to_all | solution.py:54
  60.3 12.6 %copy-start.5 = (f32[2,256]{1,0:T(2,128)S(1)}, f32[2,256]{1,0:T(2,128)}, u32[]{:S(2)}) copy-start(f32[2,256]{1,0:T(2,128)} %param.13) | copy-start | bytes 6148
  65.5 29.3 %all-to-all-start.1 = ((f32[16,1,16384]{2,1,0:T(1,128)}), f32[16,1,16384]{2,1,0:T(1,128)S(1)}, u32[]{:S(2)}, u32[]{:S(2)}) async-start(f32[16,1,16384]{2,1,0:T(1,128)} %reshape.249), calls=%async_computation.1 | async-start | bytes 2097152 | tf_op jit(solution)/shard_map/all_to_all | solution.py:56
  105.0 3.6 %copy-start.2 = (f32[2,256,256]{2,1,0:T(8,128)S(1)}, f32[2,256,256]{2,1,0:T(8,128)}, u32[]{:S(2)}) copy-start(f32[2,256,256]{2,1,0:T(8,128)} %param.11) | copy-start | bytes 1572868
  116.9 29.9 %all-to-all-start.2 = ((f32[16,1,16384]{2,1,0:T(1,128)}), f32[16,1,16384]{2,1,0:T(1,128)S(1)}, u32[]{:S(2)}, u32[]{:S(2)}) async-start(f32[16,1,16384]{2,1,0:T(1,128)} %reshape.251), calls=%async_computation.2 | async-start | bytes 2097152 | tf_op jit(solution)/shard_map/all_to_all | solution.py:69
  124.7 150.4 %all-gather.3.cloned.1.call-start = ((), (), s32[]{:S(2)}) async-start(), calls=%async_computation.4 | async-start | bytes 1081344 | tf_op jit(solution)/shard_map/all_gather | solution.py:84
  171.1 27.1 %copy-start.3 = (f32[2,32,256]{2,1,0:T(8,128)S(1)}, f32[2,32,256]{2,1,0:T(8,128)}, u32[]{:S(2)}) copy-start(f32[2,32,256]{2,1,0:T(8,128)} %param.14) | copy-start | bytes 196612
  191.9 7.8 %copy-start.6 = (f32[2,8]{1,0:T(2,128)S(1)}, f32[2,8]{1,0:T(2,128)}, u32[]{:S(2)}) copy-start(f32[2,8]{1,0:T(2,128)} %param.17) | copy-start | bytes 196
  191.9 7.8 %copy-start.7 = (s32[2,8]{1,0:T(2,128)S(1)}, s32[2,8]{1,0:T(2,128)}, u32[]{:S(2)}) copy-start(s32[2,8]{1,0:T(2,128)} %param.16) | copy-start | bytes 196
  198.2 86.7 %copy-start.4 = (f32[2,256,32]{1,2,0:T(8,128)S(1)}, f32[2,256,32]{1,2,0:T(8,128)}, u32[]{:S(2)}) copy-start(f32[2,256,32]{1,2,0:T(8,128)} %param.15) | copy-start | bytes 196612
  285.6 16.0 %copy-start.1 = (f32[2,256,256]{2,1,0:T(8,128)S(1)}, f32[2,256,256]{2,1,0:T(8,128)}, u32[]{:S(2)}) copy-start(f32[2,256,256]{2,1,0:T(8,128)} %param.12) | copy-start | bytes 1572868
Sparse Core Ops, SparseCore 0:
  199.9 75.1 all-gather.2
where the time goes:
time: 312 us; the launch traced here: 309 us
  waiting for transfers between devices  101 us (32%)
  local copies, waits for them, and re-layouts  61.8 us (20%)
  other arithmetic  50 us (16%)
  matrix products  36 us (12%)
  starting transfers between devices  25 us (8%)
  blocking collectives  20.8 us (7%)
  between operations  14.1 us (5%)
    all_gather x1, waiting for transfers between devices, on_device(): block_part = lax.all_gather(summary, 'space', axis=0, tiled=True)  75.2 us
    unnamed x30, local copies, waits for them, and re-layouts  26.5 us
    all_to_all x1, waiting for transfers between devices, on_device(): lax.all_to_all(spectrum, 'tm', split_axis=3, concat_axis=0, tiled=True)  21.9 us
    all_to_all x1, blocking collectives, on_device(): lax.all_to_all(panel_time, 'tm', split_axis=1, concat_axis=2, tiled=True)  20.8 us
    div x1, other arithmetic, inverse_table(): sine_part = -jnp.sin(phases) / step_count  17.8 us
    neg x1, other arithmetic, inverse_table(): sine_part = -jnp.sin(phases) / step_count  17.7 us
    scatter x2, local copies, waits for them, and re-layouts, on_device(): correction = jnp.zeros_like(result).at[:, :, local_index].set(result)  14.7 us
    dot_general x1, matrix products, on_device(): jnp.einsum('prqk,qtk->rtp', back_panels, backward, precision=highest)  11.4 us
  transfers between devices with their start and end apart: 4, of which 3 were waited for; matrix products, arithmetic and copies ran while one was open for 12% of the time, Pallas kernels for 0%

commit v1 on v0

v1 whole, which is shorter than its diff:
```python
import functools

import jax
import jax.numpy as jnp
from jax import lax
from jax.experimental import pallas as pl
from jax.experimental.pallas import tpu as pltpu
from jax.sharding import PartitionSpec as P

MESH = pl.DeviceIdType.MESH
RUN = 4
F32, BF16 = jnp.float32, jnp.bfloat16


def dot(a, b, dims, precision=lax.Precision.HIGHEST):
    return lax.dot_general(
        a, b, ((dims[:1], dims[1:]), ((), ())), precision=precision, preferred_element_type=F32
    )


def halves(a):
    high = a.astype(BF16)
    return high, (a - high.astype(F32)).astype(BF16)


def kernel(
    x_hbm, members_ref, v_hbm, w_hbm, lam_ref, c_hbm, e_hbm, near_ref, coup_ref, out_ref,
    x_ref, v_ref, w_ref, c_ref, e_ref, place_ref, cv_ref, ep_ref,
    ends, part_in, total_out, total_in, sum_out, sum_in, mix_out, mix_in,
    load_sem, part_send, part_recv, total_send, total_recv, sum_send, sum_recv, mix_send, mix_recv,
):
    sources, steps, panels = x_hbm.shape
    clusters, size = members_ref.shape
    rank = c_hbm.shape[1]
    rows = sources * steps
    spaces = lax.axis_size("space")
    runs = lax.axis_size("tm") // RUN
    tm, space = lax.axis_index("tm"), lax.axis_index("space")
    run, spot = tm // RUN, tm % RUN

    def run_peer(k):
        return (run * RUN + (spot + k) % RUN, space)

    def total_peer(k):
        return ((run + k) % runs * RUN + spot, space)

    def space_peer(k):
        return (tm, (space + k) % spaces)

    loads = [
        pltpu.make_async_copy(src, dst, load_sem.at[i])
        for i, (src, dst) in enumerate(
            ((x_hbm, x_ref), (w_hbm, w_ref), (v_hbm, v_ref), (c_hbm, c_ref), (e_hbm, e_ref))
        )
    ]
    for load in loads:
        load.start()

    barrier = pltpu.get_barrier_semaphore()
    for k in range(1, RUN):
        pl.semaphore_signal(barrier, inc=1, device_id=run_peer(k), device_id_type=MESH)
    for k in range(1, runs):
        pl.semaphore_signal(barrier, inc=1, device_id=total_peer(k), device_id_type=MESH)

    def greet(k, _):
        pl.semaphore_signal(barrier, inc=1, device_id=space_peer(k), device_id_type=MESH)
        return _

    lax.fori_loop(1, spaces, greet, 0)

    panel_ids = lax.broadcasted_iota(jnp.int32, (panels, size), 0) + space * panels
    for c in range(clusters):
        place_ref[c] = jnp.where(panel_ids == members_ref[c : c + 1, :], 1.0, 0.0).astype(BF16)

    lam = jnp.concatenate(
        [jnp.broadcast_to(lam_ref[c : c + 1, :], (sources, size)) for c in range(clusters)], axis=0
    )
    power = {1: 1.0 / (1.0 + lam)}
    n = 1
    while n < steps * RUN * runs:
        power[2 * n] = power[n] * power[n]
        n *= 2
    one = jnp.ones_like(lam)
    stride = [one, power[steps], power[2 * steps], power[2 * steps] * power[steps]]

    loads[0].wait()
    x_high, x_low = halves(x_ref[...].reshape(rows, panels))
    loads[1].wait()
    local = []
    for c in range(clusters):
        high = dot(x_high, place_ref[c], (1, 0), None)
        low = dot(x_low, place_ref[c], (1, 0), None)
        modes = dot(high + low, w_ref[c], (1, 1))
        own = slice(c * sources, c * sources + 1)
        first = power[1][own]
        z = (modes * first).reshape(rows // 8, 8, size)
        row = lax.broadcasted_iota(jnp.int32, (8, size), 0)
        for n in (1, 2, 4):
            z = z + jnp.where(row >= n, power[n][own], 0.0)[None] * pltpu.roll(z, n, 1)
        eight = jnp.where(row >= 4, power[4][own], 1.0) * jnp.where(row % 4 >= 2, power[2][own], 1.0)
        eight = eight * jnp.where(row % 2 >= 1, power[1][own], 1.0) * power[1][own]
        z = z.reshape(sources, steps // 8, 8, size)
        blocks = [z[:, 0]]
        for b in range(1, steps // 8):
            blocks.append(z[:, b] + eight[None] * blocks[-1][:, 7:8, :])
        local.append((blocks, eight))
        ends[c * sources : (c + 1) * sources, :] = blocks[-1][:, 7, :]

    pl.semaphore_wait(barrier, RUN - 1 + runs - 1 + spaces - 1)

    part = [
        pltpu.make_async_remote_copy(
            src_ref=ends, dst_ref=part_in.at[k - 1], send_sem=part_send.at[k - 1],
            recv_sem=part_recv.at[k - 1], device_id=run_peer(k), device_id_type=MESH,
        )
        for k in range(1, RUN)
    ]
    for copy in part:
        copy.start()

    for load in loads[2:]:
        load.wait()
    for c in range(clusters):
        cv_ref[c] = dot(c_ref[c], v_ref[c], (1, 0))
        ep_ref[c * rank : (c + 1) * rank, :] = dot(e_ref[c], place_ref[c].astype(F32), (1, 1))
    lane = lax.broadcasted_iota(jnp.int32, (1, clusters * spaces), 1)
    ids = lane % spaces * clusters + lane // spaces
    select = jnp.zeros((clusters, clusters * spaces), F32)
    for n in range(near_ref.shape[1]):
        select = select + jnp.where(near_ref[:, n : n + 1] == ids, coup_ref[:, n : n + 1], 0.0)
    select = jnp.concatenate([select[c : c + 1] for c in range(clusters)], axis=1)
    width = clusters * rows
    sum_out[:, 0, width:] = jnp.broadcast_to(select, (spaces, clusters * clusters * spaces))

    start = jnp.zeros_like(lam)
    total = jnp.zeros_like(lam)

    def stride_of(m):
        return jnp.where(m == 0, stride[0], jnp.where(m == 1, stride[1], jnp.where(m == 2, stride[2], stride[3])))

    total = ends[...] * stride_of(RUN - 1 - spot)
    for k in range(1, RUN):
        part[k - 1].wait()
        value = part_in[k - 1]
        start = start + jnp.where(spot >= k, stride[k - 1] * value, 0.0)
        total = total + stride_of(jnp.where(spot >= k, RUN - 1 - spot + k, k - 1 - spot)) * value
    total_out[...] = total
    whole = [
        pltpu.make_async_remote_copy(
            src_ref=total_out, dst_ref=total_in.at[k - 1], send_sem=total_send.at[k - 1],
            recv_sem=total_recv.at[k - 1], device_id=total_peer(k), device_id_type=MESH,
        )
        for k in range(1, runs)
    ]
    for copy in whole:
        copy.start()
    leap = power[steps * RUN]
    before = one
    carry = jnp.zeros_like(lam)
    for k in range(1, runs):
        whole[k - 1].wait()
        carry = carry + before * total_in[k - 1]
        before = before * leap
    carry = (carry + before * total) / (1.0 - power[steps * RUN * runs])
    carry = start + stride_of(spot) * carry

    solved = []
    for c in range(clusters):
        blocks, eight = local[c]
        own = slice(c * sources, (c + 1) * sources)
        step = carry[own]
        parts = []
        for b in range(steps // 8):
            parts.append(blocks[b] + eight[None] * step[:, None, :])
            step = step * power[8][own]
        y = jnp.stack(parts, axis=1).reshape(rows, size)
        solved.append(y)
        summary = dot(cv_ref[c], y, (1, 1)).astype(BF16).astype(F32)
        sum_out[:, 0, c * rows : (c + 1) * rows] = summary

    def send_sum(k, _):
        peer = space_peer(k)
        pltpu.make_async_remote_copy(
            src_ref=sum_out.at[peer[1]], dst_ref=sum_in.at[space], send_sem=sum_send,
            recv_sem=sum_recv, device_id=peer, device_id_type=MESH,
        ).start()
        return _

    lax.fori_loop(1, spaces, send_sum, 0)
    sum_in[pl.ds(space, 1)] = sum_out[pl.ds(space, 1)]

    base = None
    for c in range(clusters):
        for half in halves(dot(solved[c], v_ref[c], (1, 1))):
            term = dot(half, place_ref[c], (1, 1), None)
            base = term if base is None else base + term
    x_ref[...] = base.reshape(x_ref.shape)

    everyone = pl.ds(0, spaces - 1)
    pltpu.make_async_copy(sum_in.at[everyone], sum_in.at[everyone], sum_recv).wait()
    pltpu.make_async_copy(sum_out.at[everyone], sum_out.at[everyone], sum_send).wait()
    gathered = sum_in[...].reshape(spaces, width + clusters * clusters * spaces)
    stacked = jnp.concatenate(
        [gathered[:, c * rows : (c + 1) * rows] for c in range(clusters)], axis=0
    )
    for c in range(clusters):
        at = width + c * clusters * spaces
        mix_out[:, 0, c * rows : (c + 1) * rows] = dot(
            gathered[:, at : at + clusters * spaces], stacked, (1, 0)
        )

    def send_mix(k, _):
        peer = space_peer(k)
        pltpu.make_async_remote_copy(
            src_ref=mix_out.at[peer[1]], dst_ref=mix_in.at[space], send_sem=mix_send,
            recv_sem=mix_recv, device_id=peer, device_id_type=MESH,
        ).start()
        return _

    lax.fori_loop(1, spaces, send_mix, 0)
    mix_in[pl.ds(space, 1)] = mix_out[pl.ds(space, 1)]
    pltpu.make_async_copy(mix_in.at[everyone], mix_in.at[everyone], mix_recv).wait()
    pltpu.make_async_copy(mix_out.at[everyone], mix_out.at[everyone], mix_send).wait()

    mixed = mix_in[...].reshape(rank, width)
    mixed = jnp.concatenate([mixed[:, c * rows : (c + 1) * rows] for c in range(clusters)], axis=0)
    adjusted = dot(mixed, ep_ref[...], (0, 0))
    out_ref[...] = x_ref[...] - adjusted.reshape(out_ref.shape)


def on_device(
    residual, members, eig_vectors, eig_left, eig_values, compress, expand, neighbors, coupling
):
    sources, steps, panels = residual.shape
    clusters, size = members.shape
    rank = compress.shape[1]
    rows = sources * steps
    spaces = lax.axis_size("space")
    runs = lax.axis_size("tm") // RUN
    assert rank == spaces and steps % 8 == 0 and clusters * sources == 8
    carry = (clusters * sources, size)
    width = clusters * rows
    message = width + clusters * clusters * spaces
    anywhere, vmem = pl.BlockSpec(memory_space=pl.ANY), pl.BlockSpec(memory_space=pltpu.VMEM)
    dma = pltpu.SemaphoreType.DMA
    return pl.pallas_call(
        kernel,
        out_shape=jax.ShapeDtypeStruct(residual.shape, F32),
        in_specs=[anywhere, vmem, anywhere, anywhere, vmem, anywhere, anywhere, vmem, vmem],
        out_specs=vmem,
        scratch_shapes=[
            pltpu.VMEM(residual.shape, F32),
            pltpu.VMEM(eig_vectors.shape, F32),
            pltpu.VMEM(eig_left.shape, F32),
            pltpu.VMEM(compress.shape, F32),
            pltpu.VMEM(compress.shape, F32),
            pltpu.VMEM((clusters, panels, size), BF16),
            pltpu.VMEM((clusters, rank, size), F32),
            pltpu.VMEM((clusters * rank, panels), F32),
            pltpu.VMEM(carry, F32),
            pltpu.VMEM((RUN - 1,) + carry, F32),
            pltpu.VMEM(carry, F32),
            pltpu.VMEM((runs - 1,) + carry, F32),
            pltpu.VMEM((spaces, 1, message), F32),
            pltpu.VMEM((spaces, 1, message), F32),
            pltpu.VMEM((spaces, 1, width), F32),
            pltpu.VMEM((spaces, 1, width), F32),
            dma((5,)),
            dma((RUN - 1,)),
            dma((RUN - 1,)),
            dma((runs - 1,)),
            dma((runs - 1,)),
            dma(()),
            dma(()),
            dma(()),
            dma(()),
        ],
        compiler_params=pltpu.CompilerParams(
            collective_id=0, has_side_effects=True, vmem_limit_bytes=60 * 1024 * 1024
        ),
    )(residual, members, eig_vectors, eig_left, eig_values, compress, jnp.swapaxes(expand, 1, 2), neighbors, coupling)


def solution(mesh):
    return jax.shard_map(
        on_device,
        mesh=mesh,
        in_specs=(
            P(None, "tm", "space"),
            P("space", None),
            P("space", None, None),
            P("space", None, None),
            P("space", None),
            P("space", None, None),
            P("space", None, None),
            P("space", None),
            P("space", None),
        ),
        out_specs=P(None, "tm", "space"),
        check_vma=False,
    )
```

time: 312 us -> 50.1 us (0.16)
  waiting for transfers between devices: 101 us -> 0 us
  local copies, waits for them, and re-layouts: 61.8 us -> 1.87 us
  other arithmetic: 50 us -> 0 us
  Pallas kernels: 0 us -> 48 us
  matrix products: 36 us -> 0 us
  starting transfers between devices: 25 us -> 0 us
  blocking collectives: 20.8 us -> 0 us
  between operations: 14.1 us -> 0.01 us
    all_gather x1 -> x0, waiting for transfers between devices: 75.2 us -> none  [on_device(): block_part = lax.all_gather(summary, 'space', axis=0, tiled=True)]
    pallas_call x0 -> x1, Pallas kernels: none -> 48 us  [on_device(): pl.pallas_call(kernel, out_shape=jax.ShapeDtypeStruct(residual.shape, F32...]
    dot_general x7 -> x0, matrix products: 36 us -> none  [the longest x1 11.4 us: on_device(): jnp.einsum('prqk,qtk->rtp', back_panels, backward, precision=highest)]
    all_to_all x3 -> x0, waiting for transfers between devices: 25.9 us -> none  [the longest x1 21.9 us: on_device(): lax.all_to_all(spectrum, 'tm', split_axis=3, concat_axis=0, tiled=True)]
    all_to_all x3 -> x0, starting transfers between devices: 24.7 us -> none  [the longest x1 9.71 us: on_device(): lax.all_to_all(ordered, 'tm', split_axis=2, concat_axis=1, tiled=True)]
    unnamed x30 -> x1, local copies, waits for them, and re-layouts: 26.5 us -> 1.87 us
    all_to_all x1 -> x0, blocking collectives: 20.8 us -> none  [on_device(): lax.all_to_all(panel_time, 'tm', split_axis=1, concat_axis=2, tiled=True)]
    div x1 -> x0, other arithmetic: 17.8 us -> none  [inverse_table(): sine_part = -jnp.sin(phases) / step_count]
  transfers between devices with their start and end apart: 4 -> 0, of which waited for: 3 -> 0; matrix products, arithmetic and copies ran while one was open for 12% -> 0% of each run, Pallas kernels for 0% -> 0%
where the time goes in v1:
time: 50.1 us; the launch traced here: 49.9 us
  Pallas kernels  48 us (96%)
  local copies, waits for them, and re-layouts  1.87 us (4%)
    pallas_call x1, Pallas kernels, on_device(): pl.pallas_call(kernel, out_shape=jax.ShapeDtypeStruct(residual.shape, F32...  48 us
    unnamed x1, local copies, waits for them, and re-layouts  1.87 us

profile of v1, /device:TPU:1, one launch (start us, length us, event | category | flops | bytes accessed | tf_op | source)
XLA Modules:
  0.0 49.9 jit_solution(7258502369464428633)
XLA Ops:
  0.0 48.0 %shard_map.91 = f32[4,64,512]{2,1,0:T(8,128)} custom-call(f32[4,64,512]{2,1,0:T(8,128)} %x_hbm.1, s32[2,256]{1,0:T(2,128)} %members_ref.1, f32[2,256,256]{2,1,0:T(8,128)} %v_hbm.1, f32[2,256,256]{2,1,0:T(8,128)} %w_hbm.1, f32[2,256]{1,0:T(2,128)} %lam_ref.1, f32[2,32,256]{2,1,0:T(8,128)} %c_hbm.1, f32[2,32,256]{2,1,0:T(8,128)} %bitcast.1, s32[2,8]{1,0:T(2,128)} %near_ref.1, ...), custom_call_target="tpu_custom_call" | custom-call | tf_op jit(solution)/shard_map/pallas_call | solution.py:246
  48.0 1.9 %copy.11 = f32[4,64,512]{2,1,0:T(8,128)} copy(f32[4,64,512]{2,1,0:T(8,128)} %shard_map.91) | data formatting | bytes 1048576

commit v2 on v0

v2 whole, which is shorter than its diff:
```python
import jax
import jax.numpy as jnp
from jax import lax
from jax.experimental import pallas as pl
from jax.experimental.pallas import tpu as pltpu
from jax.sharding import PartitionSpec as P

MESH = pl.DeviceIdType.MESH
F32, BF16 = jnp.float32, jnp.bfloat16
PLANES, CORES = 4, 2
TILE, LANES = 8, 128


def dot(a, b, dims):
    return lax.dot_general(
        a, b, ((dims[:1], dims[1:]), ((), ())), preferred_element_type=F32
    )


def halves(a):
    high = a.astype(BF16)
    return high, (a - high.astype(F32)).astype(BF16)


def dot3(a, b, dims):
    return dot(a[0], b[0], dims) + (dot(a[0], b[1], dims) + dot(a[1], b[0], dims))


def kernel(
    x_hbm, members_hbm, v_hbm, w_hbm, lam_hbm, c_hbm, e_hbm, near_hbm, coup_hbm, out_ref,
    x_ref, members_ref, v_ref, w_ref, lam_ref, c_ref, e_ref, near_ref, coup_ref,
    place_ref, cv_ref, ep_ref, base_ref,
    ends, ends_in, sel_out, sel_in, sum_out, sum_in, mix_out, mix_in,
    load_sem, answer_sem, ends_send, ends_recv, sel_send, sel_recv, sum_send, sum_recv,
    mix_send, mix_recv,
):
    sources, steps, panels = x_ref.shape
    clusters, size = members_ref.shape
    rank = c_ref.shape[1]
    rows = sources * steps
    times, spaces = lax.axis_size("tm"), lax.axis_size("space")
    near = spaces // PLANES
    tm, space = lax.axis_index("tm"), lax.axis_index("space")
    plane = space // CORES % PLANES
    spot = space // (PLANES * CORES) * CORES + space % CORES
    per_block = rank // near

    def peer(at_plane, at_spot):
        return at_spot // CORES * (PLANES * CORES) + at_plane * CORES + at_spot % CORES

    def each(low, high, act):
        def body(i, _):
            act(i)
            return _

        lax.fori_loop(low, high, body, 0)

    loads = [
        pltpu.make_async_copy(src, dst, load_sem.at[i])
        for i, (src, dst) in enumerate(
            (
                (members_hbm, members_ref),
                (x_hbm, x_ref),
                (w_hbm, w_ref),
                (lam_hbm, lam_ref),
                (v_hbm, v_ref),
                (c_hbm, c_ref),
                (e_hbm, e_ref),
                (near_hbm, near_ref),
                (coup_hbm, coup_ref),
            )
        )
    ]
    for load in loads:
        load.start()

    barrier = pltpu.get_barrier_semaphore()

    def greet(device):
        pl.semaphore_signal(barrier, inc=1, device_id=device, device_id_type=MESH)

    each((plane + 1) * near, spaces, lambda i: greet((tm, peer(i // near, i % near))))
    each(1, times, lambda k: greet(((tm + k) % times, space)))
    each(1, near, lambda k: greet((tm, peer(plane, (spot + k) % near))))

    loads[0].wait()
    panel_ids = lax.broadcasted_iota(jnp.int32, (panels, size), 0) + space * panels
    for c in range(clusters):
        place_ref[c] = jnp.where(panel_ids == members_ref[c : c + 1, :], 1.0, 0.0).astype(BF16)

    loads[1].wait()
    x = halves(x_ref[...].reshape(rows, panels))
    ordered = [[dot(half, place_ref[c], (1, 0)).astype(BF16) for half in x] for c in range(clusters)]
    loads[2].wait()
    loads[3].wait()

    lam = jnp.concatenate(
        [jnp.broadcast_to(lam_ref[c : c + 1, :], (sources, size)) for c in range(clusters)], axis=0
    )
    power = {1: 1.0 / (1.0 + lam)}
    n = 1
    while n < steps * times:
        power[2 * n] = power[n] * power[n]
        n *= 2

    local = []
    for c in range(clusters):
        modes = dot3(ordered[c], halves(w_ref[c]), (1, 1))
        own = slice(c * sources, c * sources + 1)
        z = (modes * power[1][own]).reshape(rows // TILE, TILE, size)
        row = lax.broadcasted_iota(jnp.int32, (TILE, size), 0)
        ramp = power[1][own]
        for n in (1, 2, 4):
            z = z + jnp.where(row >= n, power[n][own], 0.0)[None] * pltpu.roll(z, n, 1)
            ramp = ramp * jnp.where(row // n % 2 == 1, power[n][own], 1.0)
        z = z.reshape(sources, steps // TILE, TILE, size)
        blocks = [z[:, 0]]
        for b in range(1, steps // TILE):
            blocks.append(z[:, b] + ramp[None] * blocks[-1][:, TILE - 1 :, :])
        local.append((blocks, ramp))
        ends[c * sources : (c + 1) * sources, :] = blocks[-1][:, TILE - 1, :]

    pl.semaphore_wait(barrier, times - 1 + near - 1 + plane * near)

    def copy(src, dst, send, recv, device):
        return pltpu.make_async_remote_copy(
            src_ref=src, dst_ref=dst, send_sem=send, recv_sem=recv,
            device_id=device, device_id_type=MESH,
        )

    each(
        1, times,
        lambda k: copy(ends, ends_in.at[k - 1], ends_send, ends_recv, ((tm + k) % times, space)).start(),
    )
    each(
        0, plane * near,
        lambda i: pl.semaphore_signal(
            answer_sem, inc=1, device_id=(tm, peer(i // near, i % near)), device_id_type=MESH
        ),
    )

    for load in loads[4:]:
        load.wait()
    coupled = [
        jnp.concatenate(
            [jnp.broadcast_to(ref[c : c + 1, :], (per_block, ref.shape[1])) for c in range(clusters)],
            axis=0,
        )
        for ref in (near_ref, coup_ref)
    ]
    spread = (TILE, spaces * TILE)
    lane = lax.broadcasted_iota(jnp.int32, spread, 1)
    select = jnp.zeros(spread, F32)
    for n in range(near_ref.shape[1]):
        hit = coupled[0][:, n : n + 1] == lane // per_block
        select = select + jnp.where(hit, coupled[1][:, n : n + 1], 0.0)
    same = lane % per_block == lax.broadcasted_iota(jnp.int32, spread, 0) % per_block
    sel_out[...] = jnp.where(same, select, 0.0)
    each(
        1, near,
        lambda k: copy(
            sel_out, sel_in.at[spot], sel_send, sel_recv, (tm, peer(plane, (spot + k) % near))
        ).start(),
    )
    sel_in[pl.ds(spot, 1)] = sel_out[...][None]

    cv_ref[...] = jnp.zeros_like(cv_ref)
    vectors = [halves(v_ref[c]) for c in range(clusters)]
    for c in range(clusters):
        at = slice(c * per_block, (c + 1) * per_block)
        cv = dot3(halves(c_ref[c]), vectors[c], (1, 0))
        spread_e = [dot(half, place_ref[c], (1, 1)) for half in halves(e_ref[c])]
        ep = spread_e[0] + spread_e[1]
        for b in range(near):
            block = slice(b * per_block, (b + 1) * per_block)
            cv_ref[b, at, c * size : (c + 1) * size] = cv[block]
            ep_ref[b, at, :] = ep[block]

    others = pl.ds(0, times - 1)
    pltpu.make_async_copy(ends_in.at[others], ends_in.at[others], ends_recv).wait()
    carry = ends[...]
    for k in range(times - 1, 0, -1):
        carry = carry * power[steps] + ends_in[k - 1]
    carry = carry / (1.0 - power[steps * times])

    solved = []
    for c in range(clusters):
        blocks, ramp = local[c]
        own = slice(c * sources, (c + 1) * sources)
        step = carry[own]
        parts = []
        for b in range(steps // TILE):
            parts.append(blocks[b] + ramp[None] * step[:, None, :])
            step = step * power[TILE][own]
        solved.append(halves(jnp.stack(parts, axis=1).reshape(rows, size)))
    compress = halves(cv_ref[...].reshape(rank * clusters, panels))
    summary = None
    for c in range(clusters):
        at = slice(c * size, (c + 1) * size)
        term = dot3([half[:, at] for half in compress], solved[c], (1, 1))
        summary = term if summary is None else summary + term
    summary = summary.reshape(near, TILE, rows)
    sum_out[...] = jnp.concatenate(
        [summary[:, :, i : i + LANES] for i in range(0, rows, LANES)], axis=1
    ).astype(BF16)

    def send_sum(i):
        copy(
            sum_out.at[i % near], sum_in.at[space], sum_send, sum_recv,
            (tm, peer(i // near, i % near)),
        ).start()

    each(0, plane * near, send_sum)
    each(1, near, lambda k: send_sum(plane * near + (spot + k) % near))

    @pl.when(plane < PLANES - 1)
    def _():
        pl.semaphore_wait(answer_sem, (PLANES - 1 - plane) * near)

    each((plane + 1) * near, spaces, send_sum)
    sum_in[pl.ds(space, 1)] = sum_out[pl.ds(spot, 1)]

    base = None
    for c in range(clusters):
        for half in halves(dot3(solved[c], vectors[c], (1, 1))):
            term = dot(half, place_ref[c], (1, 1))
            base = term if base is None else base + term
    base_ref[...] = base
    expand = halves(ep_ref[...].reshape(rank * clusters, panels))

    plane_peers = pl.ds(0, near - 1)
    pltpu.make_async_copy(sel_in.at[plane_peers], sel_in.at[plane_peers], sel_recv).wait()
    selector = halves(sel_in[...].reshape(near * TILE, spaces * TILE))
    everyone = pl.ds(0, spaces - 1)
    pltpu.make_async_copy(sum_in.at[everyone], sum_in.at[everyone], sum_recv).wait()
    gathered = sum_in[...].astype(F32)
    for i in range(rows // LANES):
        part = gathered[:, i * TILE : (i + 1) * TILE, :].reshape(spaces * TILE, LANES).astype(BF16)
        mixed = dot(selector[0], part, (1, 0)) + dot(selector[1], part, (1, 0))
        mix_out[:, :, i * LANES : (i + 1) * LANES] = mixed.reshape(near, TILE, LANES)

    def send_mix(k):
        to = (spot + k) % near
        copy(mix_out.at[to], mix_in.at[spot], mix_send, mix_recv, (tm, peer(plane, to))).start()

    each(1, near, send_mix)
    mix_in[pl.ds(spot, 1)] = mix_out[pl.ds(spot, 1)]
    pltpu.make_async_copy(mix_in.at[plane_peers], mix_in.at[plane_peers], mix_recv).wait()

    mixed = halves(mix_in[...].reshape(rank * clusters, rows))
    out_ref[...] = (base_ref[...] - dot3(mixed, expand, (0, 0))).reshape(out_ref.shape)

    pltpu.make_async_copy(ends_in.at[others], ends_in.at[others], ends_send).wait()
    pltpu.make_async_copy(sel_in.at[plane_peers], sel_in.at[plane_peers], sel_send).wait()
    pltpu.make_async_copy(sum_in.at[everyone], sum_in.at[everyone], sum_send).wait()
    pltpu.make_async_copy(mix_in.at[plane_peers], mix_in.at[plane_peers], mix_send).wait()


def on_device(
    residual, members, eig_vectors, eig_left, eig_values, compress, expand, neighbors, coupling
):
    sources, steps, panels = residual.shape
    clusters, size = members.shape
    rank = compress.shape[1]
    rows = sources * steps
    times, spaces = lax.axis_size("tm"), lax.axis_size("space")
    near = spaces // PLANES
    assert clusters * sources == TILE and clusters * rank == near * TILE
    assert steps % TILE == 0 and rows == 2 * LANES and clusters * size == panels
    args = (
        residual, members, eig_vectors, eig_left, eig_values, compress,
        jnp.swapaxes(expand, 1, 2), neighbors, coupling,
    )
    carry = (clusters * sources, size)
    block = (2 * TILE, LANES)
    dma = pltpu.SemaphoreType.DMA
    return pl.pallas_call(
        kernel,
        out_shape=jax.ShapeDtypeStruct(residual.shape, F32),
        in_specs=[pl.BlockSpec(memory_space=pl.ANY)] * len(args),
        out_specs=pl.BlockSpec(memory_space=pltpu.VMEM),
        scratch_shapes=[pltpu.VMEM(a.shape, a.dtype) for a in args]
        + [
            pltpu.VMEM((clusters, panels, size), BF16),
            pltpu.VMEM((near, TILE, panels), F32),
            pltpu.VMEM((near, TILE, panels), F32),
            pltpu.VMEM((rows, panels), F32),
            pltpu.VMEM(carry, F32),
            pltpu.VMEM((times - 1,) + carry, F32),
            pltpu.VMEM((TILE, spaces * TILE), F32),
            pltpu.VMEM((near, TILE, spaces * TILE), F32),
            pltpu.VMEM((near,) + block, BF16),
            pltpu.VMEM((spaces,) + block, BF16),
            pltpu.VMEM((near, TILE, rows), F32),
            pltpu.VMEM((near, TILE, rows), F32),
            dma((len(args),)),
            pltpu.SemaphoreType.REGULAR,
        ]
        + [dma(())] * 8,
        compiler_params=pltpu.CompilerParams(
            collective_id=0, has_side_effects=True, vmem_limit_bytes=60 * 1024 * 1024
        ),
    )(*args)


def solution(mesh):
    return jax.shard_map(
        on_device,
        mesh=mesh,
        in_specs=(
            P(None, "tm", "space"),
            P("space", None),
            P("space", None, None),
            P("space", None, None),
            P("space", None),
            P("space", None, None),
            P("space", None, None),
            P("space", None),
            P("space", None),
        ),
        out_specs=P(None, "tm", "space"),
        check_vma=False,
    )
```

time: 312 us -> 38.9 us (0.12); the launches traced: 309 us -> 38.8 us
  waiting for transfers between devices: 101 us -> 0 us
  local copies, waits for them, and re-layouts: 61.8 us -> 1.87 us
  other arithmetic: 50 us -> 0 us
  Pallas kernels: 0 us -> 36.9 us
  matrix products: 36 us -> 0 us
  starting transfers between devices: 25 us -> 0 us
  blocking collectives: 20.8 us -> 0 us
  between operations: 14.1 us -> 0.01 us
    all_gather x1 -> x0, waiting for transfers between devices: 75.2 us -> none  [on_device(): block_part = lax.all_gather(summary, 'space', axis=0, tiled=True)]
    pallas_call x0 -> x1, Pallas kernels: none -> 36.9 us  [on_device(): pl.pallas_call(kernel, out_shape=jax.ShapeDtypeStruct(residual.shape, F32...]
    dot_general x7 -> x0, matrix products: 36 us -> none  [the longest x1 11.4 us: on_device(): jnp.einsum('prqk,qtk->rtp', back_panels, backward, precision=highest)]
    all_to_all x3 -> x0, waiting for transfers between devices: 25.9 us -> none  [the longest x1 21.9 us: on_device(): lax.all_to_all(spectrum, 'tm', split_axis=3, concat_axis=0, tiled=True)]
    all_to_all x3 -> x0, starting transfers between devices: 24.7 us -> none  [the longest x1 9.71 us: on_device(): lax.all_to_all(ordered, 'tm', split_axis=2, concat_axis=1, tiled=True)]
    unnamed x30 -> x1, local copies, waits for them, and re-layouts: 26.5 us -> 1.87 us
    all_to_all x1 -> x0, blocking collectives: 20.8 us -> none  [on_device(): lax.all_to_all(panel_time, 'tm', split_axis=1, concat_axis=2, tiled=True)]
    div x1 -> x0, other arithmetic: 17.8 us -> none  [inverse_table(): sine_part = -jnp.sin(phases) / step_count]
  transfers between devices with their start and end apart: 4 -> 0, of which waited for: 3 -> 0; matrix products, arithmetic and copies ran while one was open for 12% -> 0% of each run, Pallas kernels for 0% -> 0%
where the time goes in v2:
time: 38.9 us; the launch traced here: 38.8 us
  Pallas kernels  36.9 us (95%)
  local copies, waits for them, and re-layouts  1.87 us (5%)
    pallas_call x1, Pallas kernels, on_device(): pl.pallas_call(kernel, out_shape=jax.ShapeDtypeStruct(residual.shape, F32...  36.9 us
    unnamed x1, local copies, waits for them, and re-layouts  1.87 us

profile of v2, /device:TPU:1, one launch (start us, length us, event | category | flops | bytes accessed | tf_op | source)
XLA Modules:
  0.0 38.8 jit_solution(4486536723034497562)
XLA Ops:
  0.0 36.9 %shard_map.91 = f32[4,64,512]{2,1,0:T(8,128)} custom-call(f32[4,64,512]{2,1,0:T(8,128)} %x_hbm.1, s32[2,256]{1,0:T(2,128)} %members_hbm.1, f32[2,256,256]{2,1,0:T(8,128)} %v_hbm.1, f32[2,256,256]{2,1,0:T(8,128)} %w_hbm.1, f32[2,256]{1,0:T(2,128)} %lam_hbm.1, f32[2,32,256]{2,1,0:T(8,128)} %c_hbm.1, f32[2,32,256]{2,1,0:T(8,128)} %bitcast.1, s32[2,8]{1,0:T(2,128)} %near_hbm.1, ...), custom_call_target="tpu_custom_call" | custom-call | tf_op jit(solution)/shard_map/pallas_call | solution.py:277
  36.9 1.9 %copy.11 = f32[4,64,512]{2,1,0:T(8,128)} copy(f32[4,64,512]{2,1,0:T(8,128)} %shard_map.91) | data formatting | bytes 1048576

commit v3 on v2

--- a/solution.py
+++ b/solution.py
@@ -8,6 +8,7 @@
 MESH = pl.DeviceIdType.MESH
 F32, BF16 = jnp.float32, jnp.bfloat16
 PLANES, CORES = 4, 2
+HUB = PLANES // 2
 TILE, LANES = 8, 128
 
 
@@ -49,6 +50,11 @@
         return at_spot // CORES * (PLANES * CORES) + at_plane * CORES + at_spot % CORES
 
     def each(low, high, act):
+        if isinstance(low, int) and isinstance(high, int):
+            for i in range(low, high):
+                act(i)
+            return
+
         def body(i, _):
             act(i)
             return _
@@ -79,7 +85,10 @@
     def greet(device):
         pl.semaphore_signal(barrier, inc=1, device_id=device, device_id_type=MESH)
 
-    each((plane + 1) * near, spaces, lambda i: greet((tm, peer(i // near, i % near))))
+    @pl.when(plane != HUB)
+    def _():
+        each(0, near, lambda k: greet((tm, peer(HUB, k))))
+
     each(1, times, lambda k: greet(((tm + k) % times, space)))
     each(1, near, lambda k: greet((tm, peer(plane, (spot + k) % near))))
 
@@ -120,7 +129,7 @@
         local.append((blocks, ramp))
         ends[c * sources : (c + 1) * sources, :] = blocks[-1][:, TILE - 1, :]
 
-    pl.semaphore_wait(barrier, times - 1 + near - 1 + plane * near)
+    pl.semaphore_wait(barrier, times - 1 + near - 1 + jnp.where(plane == HUB, spaces - near, 0))
 
     def copy(src, dst, send, recv, device):
         return pltpu.make_async_remote_copy(
@@ -132,12 +141,14 @@
         1, times,
         lambda k: copy(ends, ends_in.at[k - 1], ends_send, ends_recv, ((tm + k) % times, space)).start(),
     )
-    each(
-        0, plane * near,
-        lambda i: pl.semaphore_signal(
-            answer_sem, inc=1, device_id=(tm, peer(i // near, i % near)), device_id_type=MESH
-        ),
-    )
+
+    @pl.when(plane == HUB)
+    def _():
+        for k in range(1, PLANES):
+            pl.semaphore_signal(
+                answer_sem, inc=1, device_id=(tm, peer((HUB + k) % PLANES, spot)), device_id_type=MESH
+            )
+
 
     for load in loads[4:]:
         load.wait()
@@ -210,13 +221,12 @@
             (tm, peer(i // near, i % near)),
         ).start()
 
+    @pl.when(plane != HUB)
+    def _():
+        pl.semaphore_wait(answer_sem, 1)
+
     each(0, plane * near, send_sum)
     each(1, near, lambda k: send_sum(plane * near + (spot + k) % near))
-
-    @pl.when(plane < PLANES - 1)
-    def _():
-        pl.semaphore_wait(answer_sem, (PLANES - 1 - plane) * near)
-
     each((plane + 1) * near, spaces, send_sum)
     sum_in[pl.ds(space, 1)] = sum_out[pl.ds(spot, 1)]
 
@@ -226,7 +236,8 @@
             term = dot(half, place_ref[c], (1, 1))
             base = term if base is None else base + term
     base_ref[...] = base
-    expand = halves(ep_ref[...].reshape(rank * clusters, panels))
+    expand = halves(-ep_ref[...].reshape(rank * clusters, panels))
+    expand = jnp.concatenate([expand[0], expand[1], expand[0]], axis=0)
 
     plane_peers = pl.ds(0, near - 1)
     pltpu.make_async_copy(sel_in.at[plane_peers], sel_in.at[plane_peers], sel_recv).wait()
@@ -248,7 +259,8 @@
     pltpu.make_async_copy(mix_in.at[plane_peers], mix_in.at[plane_peers], mix_recv).wait()
 
     mixed = halves(mix_in[...].reshape(rank * clusters, rows))
-    out_ref[...] = (base_ref[...] - dot3(mixed, expand, (0, 0))).reshape(out_ref.shape)
+    mixed = jnp.concatenate([mixed[0], mixed[0], mixed[1]], axis=0)
+    out_ref[...] = (base_ref[...] + dot(mixed, expand, (0, 0))).reshape(out_ref.shape)
 
     pltpu.make_async_copy(ends_in.at[others], ends_in.at[others], ends_send).wait()
     pltpu.make_async_copy(sel_in.at[plane_peers], sel_in.at[plane_peers], sel_send).wait()
@@ -276,8 +288,8 @@
     dma = pltpu.SemaphoreType.DMA
     return pl.pallas_call(
         kernel,
-        out_shape=jax.ShapeDtypeStruct(residual.shape, F32),
-        in_specs=[pl.BlockSpec(memory_space=pl.ANY)] * len(args),
+        out_shape=pltpu.VMEM(residual.shape, F32),
+        in_specs=[pl.BlockSpec(memory_space=pltpu.HBM)] * len(args),
         out_specs=pl.BlockSpec(memory_space=pltpu.VMEM),
         scratch_shapes=[pltpu.VMEM(a.shape, a.dtype) for a in args]
         + [
@@ -298,9 +310,9 @@
         ]
         + [dma(())] * 8,
         compiler_params=pltpu.CompilerParams(
-            collective_id=0, has_side_effects=True, vmem_limit_bytes=60 * 1024 * 1024
+            collective_id=0, has_side_effects=True, vmem_limit_bytes=32 * 1024 * 1024
         ),
-    )(*args)
+    )(*(pltpu.with_memory_space_constraint(a, pltpu.HBM) for a in args))
 
 
 def solution(mesh):

time: 38.9 us -> 37.2 us (0.956)
  local copies, waits for them, and re-layouts: 1.87 us -> 0.8 us
  Pallas kernels: 36.9 us -> 36.3 us
    unnamed x1, local copies, waits for them, and re-layouts: 1.87 us -> 0.8 us
    pallas_call x1, Pallas kernels: 36.9 us -> 36.3 us  [on_device(): pl.pallas_call(kernel, out_shape=pltpu.VMEM(residual.shape, F32), in_spec...]
where the time goes in v3:
time: 37.2 us; the launch traced here: 37.1 us
  Pallas kernels  36.3 us (98%)
  local copies, waits for them, and re-layouts  0.8 us (2%)
    pallas_call x1, Pallas kernels, on_device(): pl.pallas_call(kernel, out_shape=pltpu.VMEM(residual.shape, F32), in_spec...  36.3 us
    unnamed x1, local copies, waits for them, and re-layouts  0.8 us

profile of v3, /device:TPU:1, one launch (start us, length us, event | category | flops | bytes accessed | tf_op | source)
XLA Modules:
  0.0 37.1 jit_solution(9179767647701116048)
XLA Ops:
  0.0 36.3 %shard_map.91 = f32[4,64,512]{2,1,0:T(8,128)S(1)} custom-call(f32[4,64,512]{2,1,0:T(8,128)} %x_hbm.1, s32[2,256]{1,0:T(2,128)} %members_hbm.1, f32[2,256,256]{2,1,0:T(8,128)} %v_hbm.1, f32[2,256,256]{2,1,0:T(8,128)} %w_hbm.1, f32[2,256]{1,0:T(2,128)} %lam_hbm.1, f32[2,32,256]{2,1,0:T(8,128)} %c_hbm.1, f32[2,32,256]{2,1,0:T(8,128)} %bitcast.1, ...), custom_call_target="tpu_custom_call" | custom-call | tf_op jit(solution)/shard_map/pallas_call | solution.py:289
  36.3 0.8 %copy.11 = f32[4,64,512]{2,1,0:T(8,128)} copy(f32[4,64,512]{2,1,0:T(8,128)S(1)} %shard_map.91) | data formatting | bytes 1048576

commit v4 on v3

--- a/solution.py
+++ b/solution.py
@@ -8,7 +8,9 @@
 MESH = pl.DeviceIdType.MESH
 F32, BF16 = jnp.float32, jnp.bfloat16
 PLANES, CORES = 4, 2
-HUB = PLANES // 2
+GREETED_BY = ((1, 3), (2,), (0,), (2,))
+ANSWERS = ((1, 3), (2,), (0,), (2,))
+RUN = 4
 TILE, LANES = 8, 128
 
 
@@ -61,6 +63,41 @@
 
         lax.fori_loop(low, high, body, 0)
 
+    def each_time(act):
+        runs = times // RUN
+        low = tm // RUN < runs // 2
+        for i in range(runs):
+            run = jnp.where(low, runs - 1 - i, i)
+            for turn in sorted(range(RUN), key=lambda n: -min(n, RUN - n)):
+                other = run * RUN + (tm + turn) % RUN
+                if turn or (runs > 1 and i < runs // 2):
+                    act(other)
+                else:
+                    pl.when(other != tm)(lambda other=other: act(other))
+
+    def spots(first):
+        return sorted(range(first, near), key=lambda n: -min(n // CORES, (near - n) // CORES))
+
+    def in_plane(which):
+        return pl.when(plane == which)
+
+    barrier = pltpu.get_barrier_semaphore()
+
+    def greet(device):
+        pl.semaphore_signal(barrier, inc=1, device_id=device, device_id_type=MESH)
+
+    each_time(lambda other: greet((other, space)))
+    for k in spots(1):
+        greet((tm, peer(plane, (spot + k) % near)))
+    for here in range(PLANES):
+
+        @in_plane(here)
+        def _():
+            for to in range(PLANES):
+                if here in GREETED_BY[to]:
+                    for k in spots(0):
+                        greet((tm, peer(to, (spot + k) % near)))
+
     loads = [
         pltpu.make_async_copy(src, dst, load_sem.at[i])
         for i, (src, dst) in enumerate(
@@ -80,18 +117,6 @@
     for load in loads:
         load.start()
 
-    barrier = pltpu.get_barrier_semaphore()
-
-    def greet(device):
-        pl.semaphore_signal(barrier, inc=1, device_id=device, device_id_type=MESH)
-
-    @pl.when(plane != HUB)
-    def _():
-        each(0, near, lambda k: greet((tm, peer(HUB, k))))
-
-    each(1, times, lambda k: greet(((tm + k) % times, space)))
-    each(1, near, lambda k: greet((tm, peer(plane, (spot + k) % near))))
-
     loads[0].wait()
     panel_ids = lax.broadcasted_iota(jnp.int32, (panels, size), 0) + space * panels
     for c in range(clusters):
@@ -129,7 +154,8 @@
         local.append((blocks, ramp))
         ends[c * sources : (c + 1) * sources, :] = blocks[-1][:, TILE - 1, :]
 
-    pl.semaphore_wait(barrier, times - 1 + near - 1 + jnp.where(plane == HUB, spaces - near, 0))
+    far = jnp.where(plane == 0, len(GREETED_BY[0]) * near, near)
+    pl.semaphore_wait(barrier, times - 1 + near - 1 + far)
 
     def copy(src, dst, send, recv, device):
         return pltpu.make_async_remote_copy(
@@ -137,18 +163,20 @@
             device_id=device, device_id_type=MESH,
         )
 
-    each(
-        1, times,
-        lambda k: copy(ends, ends_in.at[k - 1], ends_send, ends_recv, ((tm + k) % times, space)).start(),
-    )
-
-    @pl.when(plane == HUB)
-    def _():
-        for k in range(1, PLANES):
-            pl.semaphore_signal(
-                answer_sem, inc=1, device_id=(tm, peer((HUB + k) % PLANES, spot)), device_id_type=MESH
-            )
-
+    each_time(
+        lambda other: copy(
+            ends, ends_in.at[(other - tm + times) % times - 1], ends_send, ends_recv, (other, space)
+        ).start()
+    )
+
+    for here in range(PLANES):
+
+        @in_plane(here)
+        def _():
+            for to in ANSWERS[here]:
+                pl.semaphore_signal(
+                    answer_sem, inc=1, device_id=(tm, peer(to, spot)), device_id_type=MESH
+                )
 
     for load in loads[4:]:
         load.wait()
@@ -215,19 +243,31 @@
         [summary[:, :, i : i + LANES] for i in range(0, rows, LANES)], axis=1
     ).astype(BF16)
 
-    def send_sum(i):
-        copy(
-            sum_out.at[i % near], sum_in.at[space], sum_send, sum_recv,
-            (tm, peer(i // near, i % near)),
-        ).start()
-
-    @pl.when(plane != HUB)
-    def _():
-        pl.semaphore_wait(answer_sem, 1)
-
-    each(0, plane * near, send_sum)
-    each(1, near, lambda k: send_sum(plane * near + (spot + k) % near))
-    each((plane + 1) * near, spaces, send_sum)
+    def send_sum(to_plane, steps_on):
+        for k in steps_on:
+            to = (spot + k) % near
+            copy(
+                sum_out.at[to], sum_in.at[space], sum_send, sum_recv, (tm, peer(to_plane, to))
+            ).start()
+
+    for here in range(PLANES):
+
+        @in_plane(here)
+        def _():
+            known = GREETED_BY[here]
+            later = [to for to in range(PLANES) if to != here and to not in known]
+            if here in (1, 3):
+                known, later = (), [0, 2, 4 - here]
+            for to in known:
+                send_sum(to, spots(0))
+            if known:
+                send_sum(here, spots(1))
+            pl.semaphore_wait(answer_sem, sum(here in answers for answers in ANSWERS))
+            for to in later:
+                send_sum(to, spots(0))
+            if not known:
+                send_sum(here, spots(1))
+
     sum_in[pl.ds(space, 1)] = sum_out[pl.ds(spot, 1)]
 
     base = None
@@ -254,7 +294,8 @@
         to = (spot + k) % near
         copy(mix_out.at[to], mix_in.at[spot], mix_send, mix_recv, (tm, peer(plane, to))).start()
 
-    each(1, near, send_mix)
+    for k in spots(1):
+        send_mix(k)
     mix_in[pl.ds(spot, 1)] = mix_out[pl.ds(spot, 1)]
     pltpu.make_async_copy(mix_in.at[plane_peers], mix_in.at[plane_peers], mix_recv).wait()
 

time: 37.2 us -> 36.7 us (0.987)
  Pallas kernels: 36.3 us -> 35.7 us
    pallas_call x1, Pallas kernels: 36.3 us -> 35.7 us  [on_device(): pl.pallas_call(kernel, out_shape=pltpu.VMEM(residual.shape, F32), in_spec...]
where the time goes in v4:
time: 36.7 us; the launch traced here: 36.5 us
  Pallas kernels  35.7 us (97%)
  local copies, waits for them, and re-layouts  0.8 us (2%)
    pallas_call x1, Pallas kernels, on_device(): pl.pallas_call(kernel, out_shape=pltpu.VMEM(residual.shape, F32), in_spec...  35.7 us
    unnamed x1, local copies, waits for them, and re-layouts  0.8 us

profile of v4, /device:TPU:1, one launch (start us, length us, event | category | flops | bytes accessed | tf_op | source)
XLA Modules:
  0.0 36.5 jit_solution(13150033783237098639)
XLA Ops:
  0.0 35.7 %shard_map.91 = f32[4,64,512]{2,1,0:T(8,128)S(1)} custom-call(f32[4,64,512]{2,1,0:T(8,128)} %x_hbm.1, s32[2,256]{1,0:T(2,128)} %members_hbm.1, f32[2,256,256]{2,1,0:T(8,128)} %v_hbm.1, f32[2,256,256]{2,1,0:T(8,128)} %w_hbm.1, f32[2,256]{1,0:T(2,128)} %lam_hbm.1, f32[2,32,256]{2,1,0:T(8,128)} %c_hbm.1, f32[2,32,256]{2,1,0:T(8,128)} %bitcast.1, ...), custom_call_target="tpu_custom_call" | custom-call | tf_op jit(solution)/shard_map/pallas_call | solution.py:330
  35.7 0.8 %copy.11 = f32[4,64,512]{2,1,0:T(8,128)} copy(f32[4,64,512]{2,1,0:T(8,128)S(1)} %shard_map.91) | data formatting | bytes 1048576

commit v5 on v4

--- a/solution.py
+++ b/solution.py
@@ -8,8 +8,7 @@
 MESH = pl.DeviceIdType.MESH
 F32, BF16 = jnp.float32, jnp.bfloat16
 PLANES, CORES = 4, 2
-GREETED_BY = ((1, 3), (2,), (0,), (2,))
-ANSWERS = ((1, 3), (2,), (0,), (2,))
+EXACT = 4
 RUN = 4
 TILE, LANES = 8, 128
 
@@ -33,8 +32,8 @@
     x_hbm, members_hbm, v_hbm, w_hbm, lam_hbm, c_hbm, e_hbm, near_hbm, coup_hbm, out_ref,
     x_ref, members_ref, v_ref, w_ref, lam_ref, c_ref, e_ref, near_ref, coup_ref,
     place_ref, cv_ref, ep_ref, base_ref,
-    ends, ends_in, sel_out, sel_in, sum_out, sum_in, mix_out, mix_in,
-    load_sem, answer_sem, ends_send, ends_recv, sel_send, sel_recv, sum_send, sum_recv,
+    ends, ends_in, short, short_in, sel_out, sel_in, sum_out, sum_in, mix_out, mix_in,
+    load_sem, answer_sem, late_sem, ends_send, ends_recv, short_send, short_recv, sel_send, sel_recv, sum_send, sum_recv,
     mix_send, mix_recv,
 ):
     sources, steps, panels = x_ref.shape
@@ -76,27 +75,34 @@
                     pl.when(other != tm)(lambda other=other: act(other))
 
     def spots(first):
-        return sorted(range(first, near), key=lambda n: -min(n // CORES, (near - n) // CORES))
-
-    def in_plane(which):
-        return pl.when(plane == which)
+        return sorted(range(first, near), key=lambda n: min(n // CORES, (near - n) // CORES))
+
+    def in_planes(*which):
+        return pl.when(plane == which[0] if len(which) == 1 else plane % 2 == 1)
 
     barrier = pltpu.get_barrier_semaphore()
 
     def greet(device):
         pl.semaphore_signal(barrier, inc=1, device_id=device, device_id_type=MESH)
+
+    @in_planes(2)
+    def _():
+        greet((tm, peer(1, spot)))
+        greet((tm, peer(3, spot)))
+
+    @in_planes(1, 3)
+    def _():
+        for k in spots(0):
+            greet((tm, peer(0, (spot + k) % near)))
 
     each_time(lambda other: greet((other, space)))
     for k in spots(1):
         greet((tm, peer(plane, (spot + k) % near)))
-    for here in range(PLANES):
-
-        @in_plane(here)
-        def _():
-            for to in range(PLANES):
-                if here in GREETED_BY[to]:
-                    for k in spots(0):
-                        greet((tm, peer(to, (spot + k) % near)))
+
+    @in_planes(0)
+    def _():
+        for k in spots(0):
+            greet((tm, peer(2, (spot + k) % near)))
 
     loads = [
         pltpu.make_async_copy(src, dst, load_sem.at[i])
@@ -154,7 +160,11 @@
         local.append((blocks, ramp))
         ends[c * sources : (c + 1) * sources, :] = blocks[-1][:, TILE - 1, :]
 
-    far = jnp.where(plane == 0, len(GREETED_BY[0]) * near, near)
+    short[...] = jnp.concatenate(
+        [ends[:, i : i + LANES] for i in range(0, size, LANES)], axis=0
+    ).astype(BF16)
+
+    far = jnp.where(plane == 0, 2 * near, jnp.where(plane == 2, near, 1))
     pl.semaphore_wait(barrier, times - 1 + near - 1 + far)
 
     def copy(src, dst, send, recv, device):
@@ -163,20 +173,37 @@
             device_id=device, device_id_type=MESH,
         )
 
-    each_time(
-        lambda other: copy(
-            ends, ends_in.at[(other - tm + times) % times - 1], ends_send, ends_recv, (other, space)
-        ).start()
-    )
-
-    for here in range(PLANES):
-
-        @in_plane(here)
+    def answer(sem, to_plane):
+        pl.semaphore_signal(
+            sem, inc=1, device_id=(tm, peer(to_plane, spot)), device_id_type=MESH
+        )
+
+    @in_planes(0)
+    def _():
+        answer(answer_sem, 1)
+        answer(answer_sem, 3)
+
+    def send_ends(other):
+        back = (other - tm + times) % times
+
+        @pl.when(back > EXACT)
         def _():
-            for to in ANSWERS[here]:
-                pl.semaphore_signal(
-                    answer_sem, inc=1, device_id=(tm, peer(to, spot)), device_id_type=MESH
-                )
+            at = jnp.maximum(back - EXACT - 1, 0)
+            copy(short, short_in.at[at], short_send, short_recv, (other, space)).start()
+
+        @pl.when(back <= EXACT)
+        def _():
+            at = jnp.minimum(back - 1, EXACT - 1)
+            copy(ends, ends_in.at[at], ends_send, ends_recv, (other, space)).start()
+
+    each_time(send_ends)
+    @in_planes(1, 3)
+    def _():
+        answer(answer_sem, 2)
+
+    @in_planes(2)
+    def _():
+        answer(answer_sem, 0)
 
     for load in loads[4:]:
         load.wait()
@@ -215,11 +242,16 @@
             cv_ref[b, at, c * size : (c + 1) * size] = cv[block]
             ep_ref[b, at, :] = ep[block]
 
-    others = pl.ds(0, times - 1)
-    pltpu.make_async_copy(ends_in.at[others], ends_in.at[others], ends_recv).wait()
+    pltpu.make_async_copy(short_in, short_in, short_recv).wait()
+    pltpu.make_async_copy(ends_in, ends_in, ends_recv).wait()
     carry = ends[...]
     for k in range(times - 1, 0, -1):
-        carry = carry * power[steps] + ends_in[k - 1]
+        if k > EXACT:
+            end = short_in[k - EXACT - 1].astype(F32)
+            end = jnp.concatenate([end[i : i + TILE] for i in range(0, end.shape[0], TILE)], axis=1)
+        else:
+            end = ends_in[k - 1]
+        carry = carry * power[steps] + end
     carry = carry / (1.0 - power[steps * times])
 
     solved = []
@@ -243,30 +275,41 @@
         [summary[:, :, i : i + LANES] for i in range(0, rows, LANES)], axis=1
     ).astype(BF16)
 
-    def send_sum(to_plane, steps_on):
-        for k in steps_on:
-            to = (spot + k) % near
+    def send_sum(to_plane, to_spots):
+        for to in to_spots:
             copy(
                 sum_out.at[to], sum_in.at[space], sum_send, sum_recv, (tm, peer(to_plane, to))
             ).start()
 
-    for here in range(PLANES):
-
-        @in_plane(here)
-        def _():
-            known = GREETED_BY[here]
-            later = [to for to in range(PLANES) if to != here and to not in known]
-            if here in (1, 3):
-                known, later = (), [0, 2, 4 - here]
-            for to in known:
-                send_sum(to, spots(0))
-            if known:
-                send_sum(here, spots(1))
-            pl.semaphore_wait(answer_sem, sum(here in answers for answers in ANSWERS))
-            for to in later:
-                send_sum(to, spots(0))
-            if not known:
-                send_sum(here, spots(1))
+    def send_own():
+        send_sum(plane, [(spot + k) % near for k in spots(1)])
+
+    @in_planes(0)
+    def _():
+        send_own()
+        send_sum(1, range(near))
+        send_sum(3, range(near))
+        pl.semaphore_wait(answer_sem, 1)
+        send_sum(2, range(near))
+
+    @in_planes(1, 3)
+    def _():
+        pl.semaphore_wait(answer_sem, 1)
+        send_sum(0, range(near))
+        send_own()
+        send_sum(4 - plane, range(near))
+        pl.semaphore_wait(late_sem, 1)
+        send_sum(2, range(near))
+
+    @in_planes(2)
+    def _():
+        send_sum(0, range(near))
+        send_own()
+        pl.semaphore_wait(answer_sem, 2)
+        answer(late_sem, 1)
+        answer(late_sem, 3)
+        send_sum(1, range(near))
+        send_sum(3, range(near))
 
     sum_in[pl.ds(space, 1)] = sum_out[pl.ds(spot, 1)]
 
@@ -303,7 +346,8 @@
     mixed = jnp.concatenate([mixed[0], mixed[0], mixed[1]], axis=0)
     out_ref[...] = (base_ref[...] + dot(mixed, expand, (0, 0))).reshape(out_ref.shape)
 
-    pltpu.make_async_copy(ends_in.at[others], ends_in.at[others], ends_send).wait()
+    pltpu.make_async_copy(short_in, short_in, short_send).wait()
+    pltpu.make_async_copy(ends_in, ends_in, ends_send).wait()
     pltpu.make_async_copy(sel_in.at[plane_peers], sel_in.at[plane_peers], sel_send).wait()
     pltpu.make_async_copy(sum_in.at[everyone], sum_in.at[everyone], sum_send).wait()
     pltpu.make_async_copy(mix_in.at[plane_peers], mix_in.at[plane_peers], mix_send).wait()
@@ -319,7 +363,7 @@
     times, spaces = lax.axis_size("tm"), lax.axis_size("space")
     near = spaces // PLANES
     assert clusters * sources == TILE and clusters * rank == near * TILE
-    assert steps % TILE == 0 and rows == 2 * LANES and clusters * size == panels
+    assert steps % TILE == 0 and rows == size == 2 * LANES and clusters * size == panels
     args = (
         residual, members, eig_vectors, eig_left, eig_values, compress,
         jnp.swapaxes(expand, 1, 2), neighbors, coupling,
@@ -339,7 +383,9 @@
             pltpu.VMEM((near, TILE, panels), F32),
             pltpu.VMEM((rows, panels), F32),
             pltpu.VMEM(carry, F32),
-            pltpu.VMEM((times - 1,) + carry, F32),
+            pltpu.VMEM((EXACT,) + carry, F32),
+            pltpu.VMEM(block, BF16),
+            pltpu.VMEM((times - 1 - EXACT,) + block, BF16),
             pltpu.VMEM((TILE, spaces * TILE), F32),
             pltpu.VMEM((near, TILE, spaces * TILE), F32),
             pltpu.VMEM((near,) + block, BF16),
@@ -348,8 +394,9 @@
             pltpu.VMEM((near, TILE, rows), F32),
             dma((len(args),)),
             pltpu.SemaphoreType.REGULAR,
+            pltpu.SemaphoreType.REGULAR,
         ]
-        + [dma(())] * 8,
+        + [dma(())] * 10,
         compiler_params=pltpu.CompilerParams(
             collective_id=0, has_side_effects=True, vmem_limit_bytes=32 * 1024 * 1024
         ),

time: 36.7 us -> 34.1 us (0.929)
  Pallas kernels: 35.7 us -> 33.1 us
    pallas_call x1, Pallas kernels: 35.7 us -> 33.1 us  [on_device(): pl.pallas_call(kernel, out_shape=pltpu.VMEM(residual.shape, F32), in_spec...]
where the time goes in v5:
time: 34.1 us; the launch traced here: 34 us
  Pallas kernels  33.1 us (97%)
  local copies, waits for them, and re-layouts  0.8 us (2%)
    pallas_call x1, Pallas kernels, on_device(): pl.pallas_call(kernel, out_shape=pltpu.VMEM(residual.shape, F32), in_spec...  33.1 us
    unnamed x1, local copies, waits for them, and re-layouts  0.8 us

profile of v5, /device:TPU:1, one launch (start us, length us, event | category | flops | bytes accessed | tf_op | source)
XLA Modules:
  0.0 34.0 jit_solution(15662972907004757065)
XLA Ops:
  0.0 33.1 %shard_map.91 = f32[4,64,512]{2,1,0:T(8,128)S(1)} custom-call(f32[4,64,512]{2,1,0:T(8,128)} %x_hbm.1, s32[2,256]{1,0:T(2,128)} %members_hbm.1, f32[2,256,256]{2,1,0:T(8,128)} %v_hbm.1, f32[2,256,256]{2,1,0:T(8,128)} %w_hbm.1, f32[2,256]{1,0:T(2,128)} %lam_hbm.1, f32[2,32,256]{2,1,0:T(8,128)} %c_hbm.1, f32[2,32,256]{2,1,0:T(8,128)} %bitcast.1, ...), custom_call_target="tpu_custom_call" | custom-call | tf_op jit(solution)/shard_map/pallas_call | solution.py:374
  33.2 0.8 %copy.11 = f32[4,64,512]{2,1,0:T(8,128)} copy(f32[4,64,512]{2,1,0:T(8,128)S(1)} %shard_map.91) | data formatting | bytes 1048576

commit v6 on v5

--- a/solution.py
+++ b/solution.py
@@ -77,6 +77,8 @@
     def spots(first):
         return sorted(range(first, near), key=lambda n: min(n // CORES, (near - n) // CORES))
 
+    far_first = sorted(range(near), key=lambda n: -min(n, near - n))
+
     def in_planes(*which):
         return pl.when(plane == which[0] if len(which) == 1 else plane % 2 == 1)
 
@@ -94,15 +96,15 @@
     def _():
         for k in spots(0):
             greet((tm, peer(0, (spot + k) % near)))
+
+    @in_planes(0)
+    def _():
+        for k in spots(0):
+            greet((tm, peer(2, (spot + k) % near)))
 
     each_time(lambda other: greet((other, space)))
     for k in spots(1):
         greet((tm, peer(plane, (spot + k) % near)))
-
-    @in_planes(0)
-    def _():
-        for k in spots(0):
-            greet((tm, peer(2, (spot + k) % near)))
 
     loads = [
         pltpu.make_async_copy(src, dst, load_sem.at[i])
@@ -303,7 +305,7 @@
 
     @in_planes(2)
     def _():
-        send_sum(0, range(near))
+        send_sum(0, [(spot + k) % near for k in far_first])
         send_own()
         pl.semaphore_wait(answer_sem, 2)
         answer(late_sem, 1)
@@ -333,12 +335,12 @@
         mixed = dot(selector[0], part, (1, 0)) + dot(selector[1], part, (1, 0))
         mix_out[:, :, i * LANES : (i + 1) * LANES] = mixed.reshape(near, TILE, LANES)
 
-    def send_mix(k):
-        to = (spot + k) % near
+    def send_mix(to):
         copy(mix_out.at[to], mix_in.at[spot], mix_send, mix_recv, (tm, peer(plane, to))).start()
 
-    for k in spots(1):
-        send_mix(k)
+    for k in far_first:
+        if k:
+            send_mix((spot + k) % near)
     mix_in[pl.ds(spot, 1)] = mix_out[pl.ds(spot, 1)]
     pltpu.make_async_copy(mix_in.at[plane_peers], mix_in.at[plane_peers], mix_recv).wait()
 

time: 34.1 us -> 33.8 us (level)
  no operation moved by 1% of the time
where the time goes in v6:
time: 33.8 us; the launch traced here: 33.7 us
  Pallas kernels  32.9 us (97%)
  local copies, waits for them, and re-layouts  0.8 us (2%)
    pallas_call x1, Pallas kernels, on_device(): pl.pallas_call(kernel, out_shape=pltpu.VMEM(residual.shape, F32), in_spec...  32.9 us
    unnamed x1, local copies, waits for them, and re-layouts  0.8 us

profile of v6, /device:TPU:1, one launch (start us, length us, event | category | flops | bytes accessed | tf_op | source)
XLA Modules:
  0.0 33.7 jit_solution(10775547334867063036)
XLA Ops:
  0.0 32.9 %shard_map.91 = f32[4,64,512]{2,1,0:T(8,128)S(1)} custom-call(f32[4,64,512]{2,1,0:T(8,128)} %x_hbm.1, s32[2,256]{1,0:T(2,128)} %members_hbm.1, f32[2,256,256]{2,1,0:T(8,128)} %v_hbm.1, f32[2,256,256]{2,1,0:T(8,128)} %w_hbm.1, f32[2,256]{1,0:T(2,128)} %lam_hbm.1, f32[2,32,256]{2,1,0:T(8,128)} %c_hbm.1, f32[2,32,256]{2,1,0:T(8,128)} %bitcast.1, ...), custom_call_target="tpu_custom_call" | custom-call | tf_op jit(solution)/shard_map/pallas_call | solution.py:376
  32.9 0.8 %copy.11 = f32[4,64,512]{2,1,0:T(8,128)} copy(f32[4,64,512]{2,1,0:T(8,128)S(1)} %shard_map.91) | data formatting | bytes 1048576

commit v7 on v6

--- a/solution.py
+++ b/solution.py
@@ -224,12 +224,6 @@
         select = select + jnp.where(hit, coupled[1][:, n : n + 1], 0.0)
     same = lane % per_block == lax.broadcasted_iota(jnp.int32, spread, 0) % per_block
     sel_out[...] = jnp.where(same, select, 0.0)
-    each(
-        1, near,
-        lambda k: copy(
-            sel_out, sel_in.at[spot], sel_send, sel_recv, (tm, peer(plane, (spot + k) % near))
-        ).start(),
-    )
     sel_in[pl.ds(spot, 1)] = sel_out[...][None]
 
     cv_ref[...] = jnp.zeros_like(cv_ref)
@@ -244,6 +238,8 @@
             cv_ref[b, at, c * size : (c + 1) * size] = cv[block]
             ep_ref[b, at, :] = ep[block]
 
+    compress = halves(cv_ref[...].reshape(rank * clusters, panels))
+    round_period = 1.0 / (1.0 - power[steps * times])
     pltpu.make_async_copy(short_in, short_in, short_recv).wait()
     pltpu.make_async_copy(ends_in, ends_in, ends_recv).wait()
     carry = ends[...]
@@ -254,7 +250,7 @@
         else:
             end = ends_in[k - 1]
         carry = carry * power[steps] + end
-    carry = carry / (1.0 - power[steps * times])
+    carry = carry * round_period
 
     solved = []
     for c in range(clusters):
@@ -266,7 +262,6 @@
             parts.append(blocks[b] + ramp[None] * step[:, None, :])
             step = step * power[TILE][own]
         solved.append(halves(jnp.stack(parts, axis=1).reshape(rows, size)))
-    compress = halves(cv_ref[...].reshape(rank * clusters, panels))
     summary = None
     for c in range(clusters):
         at = slice(c * size, (c + 1) * size)
@@ -315,6 +310,12 @@
 
     sum_in[pl.ds(space, 1)] = sum_out[pl.ds(spot, 1)]
 
+    each(
+        1, near,
+        lambda k: copy(
+            sel_out, sel_in.at[spot], sel_send, sel_recv, (tm, peer(plane, (spot + k) % near))
+        ).start(),
+    )
     base = None
     for c in range(clusters):
         for half in halves(dot3(solved[c], vectors[c], (1, 1))):

time: 33.8 us -> 33.8 us (level)
  no operation moved by 1% of the time
where the time goes in v7:
time: 33.8 us; the launch traced here: 33.7 us
  Pallas kernels  32.9 us (97%)
  local copies, waits for them, and re-layouts  0.8 us (2%)
    pallas_call x1, Pallas kernels, on_device(): pl.pallas_call(kernel, out_shape=pltpu.VMEM(residual.shape, F32), in_spec...  32.9 us
    unnamed x1, local copies, waits for them, and re-layouts  0.8 us

profile of v7, /device:TPU:1, one launch (start us, length us, event | category | flops | bytes accessed | tf_op | source)
XLA Modules:
  0.0 33.7 jit_solution(9646351321870881313)
XLA Ops:
  0.0 32.9 %shard_map.91 = f32[4,64,512]{2,1,0:T(8,128)S(1)} custom-call(f32[4,64,512]{2,1,0:T(8,128)} %x_hbm.1, s32[2,256]{1,0:T(2,128)} %members_hbm.1, f32[2,256,256]{2,1,0:T(8,128)} %v_hbm.1, f32[2,256,256]{2,1,0:T(8,128)} %w_hbm.1, f32[2,256]{1,0:T(2,128)} %lam_hbm.1, f32[2,32,256]{2,1,0:T(8,128)} %c_hbm.1, f32[2,32,256]{2,1,0:T(8,128)} %bitcast.1, ...), custom_call_target="tpu_custom_call" | custom-call | tf_op jit(solution)/shard_map/pallas_call | solution.py:377
  32.9 0.8 %copy.11 = f32[4,64,512]{2,1,0:T(8,128)} copy(f32[4,64,512]{2,1,0:T(8,128)S(1)} %shard_map.91) | data formatting | bytes 1048576

commit v8 on v7

--- a/solution.py
+++ b/solution.py
@@ -279,7 +279,7 @@
             ).start()
 
     def send_own():
-        send_sum(plane, [(spot + k) % near for k in spots(1)])
+        send_sum(plane, [(spot + k) % near for k in far_first if k])
 
     @in_planes(0)
     def _():
@@ -292,7 +292,7 @@
     @in_planes(1, 3)
     def _():
         pl.semaphore_wait(answer_sem, 1)
-        send_sum(0, range(near))
+        send_sum(0, [(spot + k) % near for k in far_first])
         send_own()
         send_sum(4 - plane, range(near))
         pl.semaphore_wait(late_sem, 1)

time: 33.8 us -> 33.8 us (level)
  no operation moved by 1% of the time
where the time goes in v8:
time: 33.8 us; the launch traced here: 33.7 us
  Pallas kernels  32.9 us (97%)
  local copies, waits for them, and re-layouts  0.8 us (2%)
    pallas_call x1, Pallas kernels, on_device(): pl.pallas_call(kernel, out_shape=pltpu.VMEM(residual.shape, F32), in_spec...  32.9 us
    unnamed x1, local copies, waits for them, and re-layouts  0.8 us

profile of v8, /device:TPU:1, one launch (start us, length us, event | category | flops | bytes accessed | tf_op | source)
XLA Modules:
  0.0 33.7 jit_solution(14056780449498281247)
XLA Ops:
  0.0 32.9 %shard_map.91 = f32[4,64,512]{2,1,0:T(8,128)S(1)} custom-call(f32[4,64,512]{2,1,0:T(8,128)} %x_hbm.1, s32[2,256]{1,0:T(2,128)} %members_hbm.1, f32[2,256,256]{2,1,0:T(8,128)} %v_hbm.1, f32[2,256,256]{2,1,0:T(8,128)} %w_hbm.1, f32[2,256]{1,0:T(2,128)} %lam_hbm.1, f32[2,32,256]{2,1,0:T(8,128)} %c_hbm.1, f32[2,32,256]{2,1,0:T(8,128)} %bitcast.1, ...), custom_call_target="tpu_custom_call" | custom-call | tf_op jit(solution)/shard_map/pallas_call | solution.py:377
  32.9 0.8 %copy.11 = f32[4,64,512]{2,1,0:T(8,128)} copy(f32[4,64,512]{2,1,0:T(8,128)S(1)} %shard_map.91) | data formatting | bytes 1048576
